TPU v7x, 256 devices: a whole 4x4x8 slice. The times are simulated.
256 devices in a mesh: pipe: 8 (over z_lo, core), dp: 8 (over x, z_hi), mp: 4 (over y).
Axes of the slice: x: 4, y: 4, z: 8 (z_hi: 2, z_lo: 4; z = z_hi * 4 + z_lo), core: 2. Of those that a mesh axis runs over, the one named last changes fastest.
Arguments:
- acts: bfloat16 [16, 64, 6144], P('dp', None, 'mp'), may hold values from -6 to 6
- out_grad: bfloat16 [16, 64, 6144], P('dp', None, 'mp'), may hold values from -6 to 6
- value_weight: bfloat16 [8, 6144, 6144], P('pipe', 'dp', 'mp'), may hold values from -2 to 2
- output_weight: bfloat16 [8, 6144, 6144], P('pipe', 'mp', 'dp'), may hold values from -0.078125 to 0.078125
- decay: float32 [8, 48], P('pipe', 'mp'), may hold values from 0.6 to 0.99
Outputs:
- segment_out: bfloat16 [8, 16, 64, 6144], P('pipe', 'dp', None, 'mp')
- segment_in_grad: bfloat16 [8, 16, 64, 6144], P('pipe', 'dp', None, 'mp')
- value_grad: bfloat16 [8, 6144, 6144], P('pipe', 'dp', 'mp')
- output_grad: bfloat16 [8, 6144, 6144], P('pipe', 'mp', 'dp')
All inputs are finite; a program needn't handle non-finite values.
Results may differ from a plain program's by a relative error of at most 0.03.
Values may be sent and summed in bfloat16 or wider, within the bound.
A program may use at most 192 MiB of HBM per device.

v0:
```python
import jax
import jax.numpy as jnp
from jax import lax
from jax.sharding import PartitionSpec as P

EPSILON = 1e-05


def from_behind(value, axis, by):
    count = lax.axis_size(axis)
    pairs = [(i, i + by) for i in range(count) if 0 <= i + by < count]
    return lax.ppermute(value, axis, pairs)


def mixing_table(rates, length):
    places = jnp.arange(length).astype(jnp.float32)
    offset = places[:, None] - places[None, :]
    lower = offset >= 0.0
    powers = jnp.exp(jnp.maximum(offset, 0.0)[None, :, :] * jnp.log(rates)[:, None, None])
    scales = jnp.sqrt(1.0 - rates * rates)[:, None, None]
    return jnp.where(lower[None, :, :], powers * scales, 0.0)


def fetch_row(buffer, which):
    return lax.dynamic_index_in_dim(buffer, which, 0, keepdims=False)


def place_row(buffer, which, value, active):
    previous = fetch_row(buffer, which)
    return lax.dynamic_update_index_in_dim(buffer, jnp.where(active, value, previous), which, 0)


def mix_forward(values, table, heads_here):
    length = values.shape[0]
    spread = values.astype(jnp.float32).reshape(length, heads_here, -1)
    return jnp.einsum("hts,shd->thd", table, spread).reshape(length, -1).astype(jnp.bfloat16)


def mix_backward(grads, table, heads_here):
    length = grads.shape[0]
    spread = grads.astype(jnp.float32).reshape(length, heads_here, -1)
    return jnp.einsum("hts,thd->shd", table, spread).reshape(length, -1).astype(jnp.bfloat16)


def shards(acts, out_grad, value_weight, output_weight, decay):
    sections = lax.axis_size("pipe")
    section = lax.axis_index("pipe")
    batches, length, part = acts.shape
    weights_in, weights_out = (
        lax.all_gather(value_weight[0], "dp", axis=0, tiled=True),
        lax.all_gather(output_weight[0], "dp", axis=1, tiled=True),
    )
    width = weights_in.shape[0]
    value_width = weights_in.shape[1]
    heads_here = decay.shape[1]
    table = mixing_table(decay[0], length)
    clock = batches + sections - 1

    def forward_step(tick, carry):
        incoming, stored, normed_all, mixed_all, outputs, centers, inverses = carry
        micro = tick - section
        active = (micro >= 0) & (micro < batches)
        which = jnp.clip(micro, 0, batches - 1)
        layer_in = jnp.where(section == 0, fetch_row(acts, which), incoming)
        whole = lax.all_gather(layer_in, "mp", axis=1, tiled=True)
        floats = whole.astype(jnp.float32)
        center_mean = jnp.mean(floats, axis=1, keepdims=True)
        centered = floats - center_mean
        inverse = lax.rsqrt(jnp.mean(centered * centered, axis=1, keepdims=True) + EPSILON)
        normed = (centered * inverse).astype(jnp.bfloat16)

        def local_work(operand):
            values = jnp.dot(normed, weights_in, preferred_element_type=jnp.float32).astype(
                jnp.bfloat16
            )
            mixed = mix_forward(values, table, heads_here)
            return (jnp.dot(mixed, weights_out, preferred_element_type=jnp.float32), mixed)

        def skip_work(operand):
            return (
                jnp.zeros((length, width), jnp.float32),
                jnp.zeros((length, value_width), jnp.bfloat16),
            )

        partial_out, mixed = lax.cond(active, local_work, skip_work, 0)
        branch = lax.psum_scatter(
            partial_out.astype(jnp.bfloat16), "mp", scatter_dimension=1, tiled=True
        ).astype(jnp.float32)
        layer_out = (layer_in.astype(jnp.float32) + branch).astype(jnp.bfloat16)
        stored = place_row(stored, which, layer_in, active)
        normed_all = place_row(normed_all, which, normed, active)
        mixed_all = place_row(mixed_all, which, mixed, active)
        outputs = place_row(outputs, which, layer_out, active)
        centers = place_row(centers, which, center_mean, active)
        inverses = place_row(inverses, which, inverse, active)
        sent = from_behind(layer_out, "pipe", 1)
        return (sent, stored, normed_all, mixed_all, outputs, centers, inverses)

    start_forward = (
        jnp.zeros((length, part), jnp.bfloat16),
        jnp.zeros((batches, length, part), jnp.bfloat16),
        jnp.zeros((batches, length, width), jnp.bfloat16),
        jnp.zeros((batches, length, value_width), jnp.bfloat16),
        jnp.zeros((batches, length, part), jnp.bfloat16),
        jnp.zeros((batches, length, 1), jnp.float32),
        jnp.zeros((batches, length, 1), jnp.float32),
    )
    ended = lax.fori_loop(0, clock, forward_step, start_forward)
    stored, normed_all, mixed_all, outputs, centers, inverses = ended[1:]

    def backward_step(tick, carry):
        incoming, in_grads, value_grads, grad_wholes = carry
        micro = tick - (sections - 1 - section)
        active = (micro >= 0) & (micro < batches)
        which = jnp.clip(micro, 0, batches - 1)
        grad_in = jnp.where(section == sections - 1, fetch_row(out_grad, which), incoming)
        grad_whole = lax.all_gather(grad_in, "mp", axis=1, tiled=True)

        def local_back(operand):
            mixed_grad = jnp.einsum(
                "tw,vw->tv", grad_whole, weights_out, preferred_element_type=jnp.float32
            ).astype(jnp.bfloat16)
            values_grad = mix_backward(mixed_grad, table, heads_here)
            return (
                jnp.einsum(
                    "tv,wv->tw", values_grad, weights_in, preferred_element_type=jnp.float32
                ),
                values_grad,
            )

        def skip_back(operand):
            return (
                jnp.zeros((length, width), jnp.float32),
                jnp.zeros((length, value_width), jnp.bfloat16),
            )

        partial_grad, values_grad = lax.cond(active, local_back, skip_back, 0)
        normed_grad = lax.psum_scatter(
            partial_grad.astype(jnp.bfloat16), "mp", scatter_dimension=1, tiled=True
        ).astype(jnp.float32)
        inverse = fetch_row(inverses, which)
        scaled = (
            fetch_row(stored, which).astype(jnp.float32) - fetch_row(centers, which)
        ) * inverse
        first_sum, second_sum = lax.psum(
            (jnp.sum(normed_grad, axis=1), jnp.sum(normed_grad * scaled, axis=1)), "mp"
        )
        hidden_grad = inverse * (
            normed_grad - first_sum[:, None] / width - scaled * (second_sum[:, None] / width)
        )
        grad_out = (grad_in.astype(jnp.float32) + hidden_grad).astype(jnp.bfloat16)
        in_grads = place_row(in_grads, which, grad_out, active)
        value_grads = place_row(value_grads, which, values_grad, active)
        grad_wholes = place_row(grad_wholes, which, grad_whole, active)
        sent = from_behind(grad_out, "pipe", -1)
        return (sent, in_grads, value_grads, grad_wholes)

    start_backward = (
        jnp.zeros((length, part), jnp.bfloat16),
        jnp.zeros((batches, length, part), jnp.bfloat16),
        jnp.zeros((batches, length, value_width), jnp.bfloat16),
        jnp.zeros((batches, length, width), jnp.bfloat16),
    )
    finished = lax.fori_loop(0, clock, backward_step, start_backward)
    in_grads, value_grads, grad_wholes = finished[1:]
    normed_rows = normed_all.reshape(-1, width)
    mixed_rows = mixed_all.reshape(-1, value_width)
    value_rows = value_grads.reshape(-1, value_width)
    grad_rows = grad_wholes.reshape(-1, width)
    normed_cols, grad_cols = (
        lax.all_to_all(normed_rows, "dp", split_axis=1, concat_axis=0, tiled=True),
        lax.all_to_all(grad_rows, "dp", split_axis=1, concat_axis=0, tiled=True),
    )
    value_all, mixed_all_rows = (
        lax.all_gather(value_rows, "dp", axis=0, tiled=True),
        lax.all_gather(mixed_rows, "dp", axis=0, tiled=True),
    )
    value_sum = jnp.einsum("tr,tv->rv", normed_cols, value_all, preferred_element_type=jnp.float32)
    output_sum = jnp.einsum(
        "tv,tw->vw", mixed_all_rows, grad_cols, preferred_element_type=jnp.float32
    )
    return (
        outputs[None],
        in_grads[None],
        value_sum.astype(jnp.bfloat16)[None],
        output_sum.astype(jnp.bfloat16)[None],
    )


def solution(mesh):
    in_specs = (
        P("dp", None, "mp"),
        P("dp", None, "mp"),
        P("pipe", "dp", "mp"),
        P("pipe", "mp", "dp"),
        P("pipe", "mp"),
    )
    out_specs = (
        P("pipe", "dp", None, "mp"),
        P("pipe", "dp", None, "mp"),
        P("pipe", "dp", "mp"),
        P("pipe", "mp", "dp"),
    )
    return jax.shard_map(shards, mesh=mesh, in_specs=in_specs, out_specs=out_specs, check_vma=False)
```

profile of v0, /device:TPU:134, one launch (start us, length us, event | category | flops | bytes accessed | tf_op | source)
XLA Modules:
  0.0 2224.9 jit_solution(114284665566799888)
XLA Ops:
  10.8 335.2 %all-gather.11.cloned.1.call-done = bf16[1,6144,1536]{2,1,0:T(8,128)(2,1)} async-done(((bf16[1,768,1536]{2,1,0:T(8,128)(2,1)}), bf16[1,6144,1536]{2,1,0:T(8,128)(2,1)}) %all-gather.11.cloned.1.call-update) | async-done | bytes 18874384 | tf_op jit(solution)/shard_map/all_gather | solution.py:50
  345.9 336.0 %all-gather.13.cloned.1.call-done = bf16[1,1536,6144]{2,1,0:T(8,128)(2,1)} async-done(((bf16[1,1536,768]{2,1,0:T(8,128)(2,1)}), bf16[1,1536,6144]{2,1,0:T(8,128)(2,1)}) %all-gather.13.cloned.1.call-update) | async-done | bytes 18874384 | tf_op jit(solution)/shard_map/all_gather | solution.py:51
  684.1 577.2 %while.49 = (s32[]{:T(128)}, bf16[64,1536]{1,0:T(8,128)(2,1)S(1)}, bf16[2,64,1536]{2,1,0:T(8,128)(2,1)S(1)}, bf16[2,64,6144]{2,1,0:T(8,128)(2,1)S(1)}, bf16[2,64...) while((s32[]{:T(128)}, bf16[64,1536]{1,0:T(8,128)(2,1)S(1)}, ...), condition=%wide.region_6.7_spmd.clone, body=%wide.region_0.6_spmd.clone.sunk | while | flops 2433859840 | bytes 134007752 | solution.py:108
  700.4 16.2 conditional.6
  719.6 24.9 %reduce-scatter.3.cloned.1.call-done = bf16[64,1536]{1,0:T(8,128)(2,1)} async-done(((bf16[64,6144]{1,0:T(8,128)(2,1)}), bf16[64,1536]{1,0:T(8,128)(2,1)}) %reduce-scatter.3.cloned.1.call-update) | async-done | bytes 196624 | tf_op jit(solution)/shard_map/while/body/eval_jaxpr/reduce_scatter | solution.py:86
  764.9 16.2 conditional.6
  784.0 23.5 %reduce-scatter.3.cloned.1.call-done = bf16[64,1536]{1,0:T(8,128)(2,1)} async-done(((bf16[64,6144]{1,0:T(8,128)(2,1)}), bf16[64,1536]{1,0:T(8,128)(2,1)}) %reduce-scatter.3.cloned.1.call-update) | async-done | bytes 196624 | tf_op jit(solution)/shard_map/while/body/eval_jaxpr/reduce_scatter | solution.py:86
  830.7 42.6 %reduce-scatter.3.cloned.1.call-done = bf16[64,1536]{1,0:T(8,128)(2,1)} async-done(((bf16[64,6144]{1,0:T(8,128)(2,1)}), bf16[64,1536]{1,0:T(8,128)(2,1)}) %reduce-scatter.3.cloned.1.call-update) | async-done | bytes 196624 | tf_op jit(solution)/shard_map/while/body/eval_jaxpr/reduce_scatter | solution.py:86
  896.4 42.7 %reduce-scatter.3.cloned.1.call-done = bf16[64,1536]{1,0:T(8,128)(2,1)} async-done(((bf16[64,6144]{1,0:T(8,128)(2,1)}), bf16[64,1536]{1,0:T(8,128)(2,1)}) %reduce-scatter.3.cloned.1.call-update) | async-done | bytes 196624 | tf_op jit(solution)/shard_map/while/body/eval_jaxpr/reduce_scatter | solution.py:86
  962.2 41.9 %reduce-scatter.3.cloned.1.call-done = bf16[64,1536]{1,0:T(8,128)(2,1)} async-done(((bf16[64,6144]{1,0:T(8,128)(2,1)}), bf16[64,1536]{1,0:T(8,128)(2,1)}) %reduce-scatter.3.cloned.1.call-update) | async-done | bytes 196624 | tf_op jit(solution)/shard_map/while/body/eval_jaxpr/reduce_scatter | solution.py:86
  1027.2 41.8 %reduce-scatter.3.cloned.1.call-done = bf16[64,1536]{1,0:T(8,128)(2,1)} async-done(((bf16[64,6144]{1,0:T(8,128)(2,1)}), bf16[64,1536]{1,0:T(8,128)(2,1)}) %reduce-scatter.3.cloned.1.call-update) | async-done | bytes 196624 | tf_op jit(solution)/shard_map/while/body/eval_jaxpr/reduce_scatter | solution.py:86
  1092.2 41.8 %reduce-scatter.3.cloned.1.call-done = bf16[64,1536]{1,0:T(8,128)(2,1)} async-done(((bf16[64,6144]{1,0:T(8,128)(2,1)}), bf16[64,1536]{1,0:T(8,128)(2,1)}) %reduce-scatter.3.cloned.1.call-update) | async-done | bytes 196624 | tf_op jit(solution)/shard_map/while/body/eval_jaxpr/reduce_scatter | solution.py:86
  1157.1 42.0 %reduce-scatter.3.cloned.1.call-done = bf16[64,1536]{1,0:T(8,128)(2,1)} async-done(((bf16[64,6144]{1,0:T(8,128)(2,1)}), bf16[64,1536]{1,0:T(8,128)(2,1)}) %reduce-scatter.3.cloned.1.call-update) | async-done | bytes 196624 | tf_op jit(solution)/shard_map/while/body/eval_jaxpr/reduce_scatter | solution.py:86
  1222.1 35.1 %reduce-scatter.3.cloned.1.call-done = bf16[64,1536]{1,0:T(8,128)(2,1)} async-done(((bf16[64,6144]{1,0:T(8,128)(2,1)}), bf16[64,1536]{1,0:T(8,128)(2,1)}) %reduce-scatter.3.cloned.1.call-update) | async-done | bytes 196624 | tf_op jit(solution)/shard_map/while/body/eval_jaxpr/reduce_scatter | solution.py:86
  1264.2 728.4 %while.50 = (s32[]{:T(128)}, bf16[64,1536]{1,0:T(8,128)(2,1)S(1)}, bf16[2,64,1536]{2,1,0:T(8,128)(2,1)}, bf16[2,64,1536]{2,1,0:T(8,128)(2,1)}, bf16[2,64,6144]{2...) while((s32[]{:T(128)}, bf16[64,1536]{1,0:T(8,128)(2,1)S(1)}, ...), condition=%wide.region_15.16_spmd.clone, body=%wide.region_7.15_spmd.clone.sunk | while | flops 2431205376 | bytes 59074636 | solution.py:164
  1285.2 41.2 %reduce-scatter.5.cloned.1.call-done = bf16[64,1536]{1,0:T(8,128)(2,1)} async-done(((bf16[64,6144]{1,0:T(8,128)(2,1)}), bf16[64,1536]{1,0:T(8,128)(2,1)}) %reduce-scatter.5.cloned.1.call-update) | async-done | bytes 196624 | tf_op jit(solution)/shard_map/while/body/eval_jaxpr/reduce_scatter | solution.py:138
  1342.1 14.0 all_gather.38
  1362.1 45.2 %reduce-scatter.5.cloned.1.call-done = bf16[64,1536]{1,0:T(8,128)(2,1)} async-done(((bf16[64,6144]{1,0:T(8,128)(2,1)}), bf16[64,1536]{1,0:T(8,128)(2,1)}) %reduce-scatter.5.cloned.1.call-update) | async-done | bytes 196624 | tf_op jit(solution)/shard_map/while/body/eval_jaxpr/reduce_scatter | solution.py:138
  1442.9 45.3 %reduce-scatter.5.cloned.1.call-done = bf16[64,1536]{1,0:T(8,128)(2,1)} async-done(((bf16[64,6144]{1,0:T(8,128)(2,1)}), bf16[64,1536]{1,0:T(8,128)(2,1)}) %reduce-scatter.5.cloned.1.call-update) | async-done | bytes 196624 | tf_op jit(solution)/shard_map/while/body/eval_jaxpr/reduce_scatter | solution.py:138
  1503.8 14.1 all_gather.38
  1523.7 46.0 %reduce-scatter.5.cloned.1.call-done = bf16[64,1536]{1,0:T(8,128)(2,1)} async-done(((bf16[64,6144]{1,0:T(8,128)(2,1)}), bf16[64,1536]{1,0:T(8,128)(2,1)}) %reduce-scatter.5.cloned.1.call-update) | async-done | bytes 196624 | tf_op jit(solution)/shard_map/while/body/eval_jaxpr/reduce_scatter | solution.py:138
  1605.2 45.9 %reduce-scatter.5.cloned.1.call-done = bf16[64,1536]{1,0:T(8,128)(2,1)} async-done(((bf16[64,6144]{1,0:T(8,128)(2,1)}), bf16[64,1536]{1,0:T(8,128)(2,1)}) %reduce-scatter.5.cloned.1.call-update) | async-done | bytes 196624 | tf_op jit(solution)/shard_map/while/body/eval_jaxpr/reduce_scatter | solution.py:138
  1686.7 46.8 %reduce-scatter.5.cloned.1.call-done = bf16[64,1536]{1,0:T(8,128)(2,1)} async-done(((bf16[64,6144]{1,0:T(8,128)(2,1)}), bf16[64,1536]{1,0:T(8,128)(2,1)}) %reduce-scatter.5.cloned.1.call-update) | async-done | bytes 196624 | tf_op jit(solution)/shard_map/while/body/eval_jaxpr/reduce_scatter | solution.py:138
  1749.2 14.1 all_gather.38
  1769.1 46.7 %reduce-scatter.5.cloned.1.call-done = bf16[64,1536]{1,0:T(8,128)(2,1)} async-done(((bf16[64,6144]{1,0:T(8,128)(2,1)}), bf16[64,1536]{1,0:T(8,128)(2,1)}) %reduce-scatter.5.cloned.1.call-update) | async-done | bytes 196624 | tf_op jit(solution)/shard_map/while/body/eval_jaxpr/reduce_scatter | solution.py:138
  1845.5 25.4 %conditional.7 = (bf16[64,6144]{1,0:T(8,128)(2,1)S(1)}, bf16[64,1536]{1,0:T(8,128)(2,1)}) conditional(s32[]{:T(128)} %convert_element_type.240, () %tuple.124, (bf16[64,6144]{1,0:T(8,128)(2,1)S(1)}, bf16[1536,6144]{1,0:T(8,128)(2,1)}, pred[64,64]{0,1:T(8,128)(4,1)S(1)}, bf16[6144,1536]{1,0:T(8,128)(2,1)}, f32[64,64]{0,1:T(8,128)}, ...), branch_computations={%region_8.8_spmd, %region_9.9_spmd} | conditional | flops 2428747776 | bytes 40587848 | solution.py:137
  1876.1 20.9 reduce-scatter.5.cloned.1.call-done
  1926.7 25.4 %conditional.7 = (bf16[64,6144]{1,0:T(8,128)(2,1)S(1)}, bf16[64,1536]{1,0:T(8,128)(2,1)}) conditional(s32[]{:T(128)} %convert_element_type.240, () %tuple.124, (bf16[64,6144]{1,0:T(8,128)(2,1)S(1)}, bf16[1536,6144]{1,0:T(8,128)(2,1)}, pred[64,64]{0,1:T(8,128)(4,1)S(1)}, bf16[6144,1536]{1,0:T(8,128)(2,1)}, f32[64,64]{0,1:T(8,128)}, ...), branch_computations={%region_8.8_spmd, %region_9.9_spmd} | conditional | flops 2428747776 | bytes 40587848 | solution.py:137
  1957.3 20.7 reduce-scatter.5.cloned.1.call-done
  2008.6 23.6 %all-to-all-done.1 = bf16[128,8,768]{2,0,1:T(8,128)(2,1)S(1)} async-done(((bf16[128,8,768]{2,0,1:T(8,128)(2,1)}), bf16[128,8,768]{2,0,1:T(8,128)(2,1)S(1)}, u32[]{:S(2)}, u32[]{:S(2)}) %all-to-all-start.1) | async-done | bytes 1572896 | tf_op jit(solution)/shard_map/all_to_all | solution.py:172
  2041.5 88.0 %all-gather.9.cloned.1.call-done = bf16[1024,1536]{1,0:T(8,128)(2,1)} async-done(((bf16[128,1536]{1,0:T(8,128)(2,1)}), bf16[1024,1536]{1,0:T(8,128)(2,1)}) %all-gather.9.cloned.1.call-update) | async-done | bytes 3145744 | tf_op jit(solution)/shard_map/all_gather | solution.py:176
  2135.4 76.9 %all-gather.7.cloned.1.call-done = bf16[1024,1536]{1,0:T(8,128)(2,1)} async-done(((bf16[128,1536]{1,0:T(8,128)(2,1)}), bf16[1024,1536]{1,0:T(8,128)(2,1)}) %all-gather.7.cloned.1.call-update) | async-done | bytes 3145744 | tf_op jit(solution)/shard_map/all_gather | solution.py:175
  (646 shorter events, 622.1 us)
Async XLA Ops:
  7.2 338.8 %all-gather.11.cloned.1.call-start = ((), (), s32[]{:S(2)}) async-start(), calls=%async_computation.6 | async-start | bytes 21233664 | tf_op jit(solution)/shard_map/all_gather | solution.py:50
  7.9 674.0 %all-gather.13.cloned.1.call-start = ((), (), s32[]{:S(2)}) async-start(), calls=%async_computation.7 | async-start | bytes 21233664 | tf_op jit(solution)/shard_map/all_gather | solution.py:51
  684.1 60.4 %reduce-scatter.3.cloned.1.call-start = ((), (), s32[]{:S(2)}) async-start(), calls=%async_computation.8 | async-start | bytes 983040 | tf_op jit(solution)/shard_map/while/body/eval_jaxpr/reduce_scatter | solution.py:86
  748.5 59.0 %reduce-scatter.3.cloned.1.call-start = ((), (), s32[]{:S(2)}) async-start(), calls=%async_computation.8 | async-start | bytes 983040 | tf_op jit(solution)/shard_map/while/body/eval_jaxpr/reduce_scatter | solution.py:86
  811.6 61.7 %reduce-scatter.3.cloned.1.call-start = ((), (), s32[]{:S(2)}) async-start(), calls=%async_computation.8 | async-start | bytes 983040 | tf_op jit(solution)/shard_map/while/body/eval_jaxpr/reduce_scatter | solution.py:86
  877.3 61.8 %reduce-scatter.3.cloned.1.call-start = ((), (), s32[]{:S(2)}) async-start(), calls=%async_computation.8 | async-start | bytes 983040 | tf_op jit(solution)/shard_map/while/body/eval_jaxpr/reduce_scatter | solution.py:86
  943.2 61.0 %reduce-scatter.3.cloned.1.call-start = ((), (), s32[]{:S(2)}) async-start(), calls=%async_computation.8 | async-start | bytes 983040 | tf_op jit(solution)/shard_map/while/body/eval_jaxpr/reduce_scatter | solution.py:86
  1008.2 60.9 %reduce-scatter.3.cloned.1.call-start = ((), (), s32[]{:S(2)}) async-start(), calls=%async_computation.8 | async-start | bytes 983040 | tf_op jit(solution)/shard_map/while/body/eval_jaxpr/reduce_scatter | solution.py:86
  1073.1 60.9 %reduce-scatter.3.cloned.1.call-start = ((), (), s32[]{:S(2)}) async-start(), calls=%async_computation.8 | async-start | bytes 983040 | tf_op jit(solution)/shard_map/while/body/eval_jaxpr/reduce_scatter | solution.py:86
  1138.0 61.0 %reduce-scatter.3.cloned.1.call-start = ((), (), s32[]{:S(2)}) async-start(), calls=%async_computation.8 | async-start | bytes 983040 | tf_op jit(solution)/shard_map/while/body/eval_jaxpr/reduce_scatter | solution.py:86
  1203.1 54.2 %reduce-scatter.3.cloned.1.call-start = ((), (), s32[]{:S(2)}) async-start(), calls=%async_computation.8 | async-start | bytes 983040 | tf_op jit(solution)/shard_map/while/body/eval_jaxpr/reduce_scatter | solution.py:86
  1264.4 62.0 %reduce-scatter.5.cloned.1.call-start = ((), (), s32[]{:S(2)}) async-start(), calls=%async_computation.9 | async-start | bytes 983040 | tf_op jit(solution)/shard_map/while/body/eval_jaxpr/reduce_scatter | solution.py:138
  1337.7 3.3 collective-permute-start.1
  1341.0 66.2 %reduce-scatter.5.cloned.1.call-start = ((), (), s32[]{:S(2)}) async-start(), calls=%async_computation.9 | async-start | bytes 983040 | tf_op jit(solution)/shard_map/while/body/eval_jaxpr/reduce_scatter | solution.py:138
  1418.6 3.3 collective-permute-start.1
  1421.9 66.3 %reduce-scatter.5.cloned.1.call-start = ((), (), s32[]{:S(2)}) async-start(), calls=%async_computation.9 | async-start | bytes 983040 | tf_op jit(solution)/shard_map/while/body/eval_jaxpr/reduce_scatter | solution.py:138
  1499.3 3.3 collective-permute-start.1
  1502.7 67.0 %reduce-scatter.5.cloned.1.call-start = ((), (), s32[]{:S(2)}) async-start(), calls=%async_computation.9 | async-start | bytes 983040 | tf_op jit(solution)/shard_map/while/body/eval_jaxpr/reduce_scatter | solution.py:138
  1580.9 3.3 collective-permute-start.1
  1584.2 66.9 %reduce-scatter.5.cloned.1.call-start = ((), (), s32[]{:S(2)}) async-start(), calls=%async_computation.9 | async-start | bytes 983040 | tf_op jit(solution)/shard_map/while/body/eval_jaxpr/reduce_scatter | solution.py:138
  1662.4 3.3 collective-permute-start.1
  1665.7 67.8 %reduce-scatter.5.cloned.1.call-start = ((), (), s32[]{:S(2)}) async-start(), calls=%async_computation.9 | async-start | bytes 983040 | tf_op jit(solution)/shard_map/while/body/eval_jaxpr/reduce_scatter | solution.py:138
  1744.7 3.3 collective-permute-start.1
  1748.1 67.7 %reduce-scatter.5.cloned.1.call-start = ((), (), s32[]{:S(2)}) async-start(), calls=%async_computation.9 | async-start | bytes 983040 | tf_op jit(solution)/shard_map/while/body/eval_jaxpr/reduce_scatter | solution.py:138
  1827.1 3.3 collective-permute-start.1
  1830.4 66.6 %reduce-scatter.5.cloned.1.call-start = ((), (), s32[]{:S(2)}) async-start(), calls=%async_computation.9 | async-start | bytes 983040 | tf_op jit(solution)/shard_map/while/body/eval_jaxpr/reduce_scatter | solution.py:138
  1908.2 3.3 collective-permute-start.1
  1911.5 66.4 %reduce-scatter.5.cloned.1.call-start = ((), (), s32[]{:S(2)}) async-start(), calls=%async_computation.9 | async-start | bytes 983040 | tf_op jit(solution)/shard_map/while/body/eval_jaxpr/reduce_scatter | solution.py:138
  1992.6 136.9 %all-gather.9.cloned.1.call-start = ((), (), s32[]{:S(2)}) async-start(), calls=%async_computation.5 | async-start | bytes 3538944 | tf_op jit(solution)/shard_map/all_gather | solution.py:176
  1996.5 35.7 %all-to-all-start.1 = ((bf16[128,8,768]{2,0,1:T(8,128)(2,1)}), bf16[128,8,768]{2,0,1:T(8,128)(2,1)S(1)}, u32[]{:S(2)}, u32[]{:S(2)}) async-start(bf16[128,8,768]{2,0,1:T(8,128)(2,1)} %copy.34), calls=%async_computation.3 | async-start | bytes 3145728 | tf_op jit(solution)/shard_map/all_to_all | solution.py:172
  2006.1 206.2 %all-gather.7.cloned.1.call-start = ((), (), s32[]{:S(2)}) async-start(), calls=%async_computation.4 | async-start | bytes 3538944 | tf_op jit(solution)/shard_map/all_gather | solution.py:175
  2032.2 103.2 %all-to-all-start = ((bf16[128,8,768]{2,0,1:T(8,128)(2,1)}), bf16[128,8,768]{2,0,1:T(8,128)(2,1)S(1)}, u32[]{:S(2)}, u32[]{:S(2)}) async-start(bf16[128,8,768]{2,0,1:T(8,128)(2,1)} %copy.33), calls=%async_computation.2 | async-start | bytes 3145728 | tf_op jit(solution)/shard_map/all_to_all | solution.py:171
  (131 other events, 2129.1 us)
Sparse Core Ops, SparseCore 0:
  10.6 335.2 all-gather.10
  348.5 333.2 all-gather.12
  717.7 26.7 reduce-scatter.2
  782.2 25.3 reduce-scatter.2
  829.7 43.5 reduce-scatter.2
  895.5 43.6 reduce-scatter.2
  961.3 42.7 reduce-scatter.2
  1026.3 42.7 reduce-scatter.2
  1091.2 42.6 reduce-scatter.2
  1156.1 42.8 reduce-scatter.2
  1221.2 36.0 reduce-scatter.2
  1281.1 45.2 reduce-scatter.4
  1358.0 49.2 reduce-scatter.4
  1438.8 49.3 reduce-scatter.4
  1519.6 50.0 reduce-scatter.4
  1601.1 49.9 reduce-scatter.4
  1682.6 50.8 reduce-scatter.4
  1765.0 50.7 reduce-scatter.4
  1872.0 24.9 reduce-scatter.4
  1953.1 24.7 reduce-scatter.4
  1996.0 133.4 all-gather.8
  2132.1 80.1 all-gather.6
where the time goes:
time: 2240 us; the launch traced here: 2220 us
  waiting for transfers between devices  1580 us (71%)
  blocking collectives  324 us (14%)
  other arithmetic  92.3 us (4%)
  matrix products  90.1 us (4%)
  local copies, waits for them, and re-layouts  83 us (4%)
  starting transfers between devices  42.2 us (2%)
    reduce_scatter x9, waiting for transfers between devices, backward_step(): lax.psum_scatter(partial_grad.astype(jnp.bfloat16), 'mp', scatter_dimensi...  359 us
    reduce_scatter x9, waiting for transfers between devices, forward_step(): lax.psum_scatter(partial_out.astype(jnp.bfloat16), 'mp', scatter_dimensio...  336 us
    all_gather x1, waiting for transfers between devices, shards(): lax.all_gather(output_weight[0], 'dp', axis=1, tiled=True)  336 us
    all_gather x1, waiting for transfers between devices, shards(): lax.all_gather(value_weight[0], 'dp', axis=0, tiled=True)  335 us
    all_gather x9, blocking collectives, backward_step(): grad_whole = lax.all_gather(grad_in, 'mp', axis=1, tiled=True)  126 us
    all_gather x9, blocking collectives, forward_step(): whole = lax.all_gather(layer_in, 'mp', axis=1, tiled=True)  125 us
    all_gather x1, waiting for transfers between devices, shards(): lax.all_gather(mixed_rows, 'dp', axis=0, tiled=True)  88 us
    all_gather x1, waiting for transfers between devices, shards(): lax.all_gather(value_rows, 'dp', axis=0, tiled=True)  76.9 us
  transfers between devices with their start and end apart: 42, of which 41 were waited for; matrix products, arithmetic and copies ran while one was open for 3% of the time, Pallas kernels for 0%

commit v1 on v0

v1 whole, which is shorter than its diff:
```python
import functools

import jax
import jax.numpy as jnp
from jax import lax
from jax.experimental import pallas as pl
from jax.experimental.pallas import tpu as pltpu
from jax.sharding import PartitionSpec as P

EPSILON = 1e-05
F32 = jnp.float32
BF16 = jnp.bfloat16
MESH = pl.DeviceIdType.MESH

TOKENS = 1024
MBT = 64
ROWS = 64
CHUNKS = TOKENS // ROWS
OWN = ROWS // 4
WIDTH = 6144
BLK = 768
VAL = 1536
PIECE = 384
SECTIONS = 8
LANES = 128

FORWARD_ORDER = ((1, 0), (3, 1), (5, 2), (2, 0), (4, 1))
BACKWARD_ORDER = ((1, 0), (3, 1), (5, 2), (2, 0), (4, 1))


def send(src, dst, send_sem, recv_sem, **device):
    pltpu.make_async_remote_copy(
        src_ref=src,
        dst_ref=dst,
        send_sem=send_sem,
        recv_sem=recv_sem,
        device_id=device,
        device_id_type=MESH,
    ).start()


def await_bytes(ref, sem):
    pltpu.make_async_copy(ref, ref, sem).wait()


def send_or_copy(here, src, dst, send_sem, recv_sem, **device):
    @pl.when(here)
    def _():
        pltpu.make_async_copy(src, dst, recv_sem).start()

    @pl.when(jnp.logical_not(here))
    def _():
        send(src, dst, send_sem, recv_sem, **device)


def run_phases(order, phases):
    last = max(lag for _, lag in order)

    def window(step, carry):
        for which, lag in order:
            chunk = step - lag
            pl.when((chunk >= 0) & (chunk < CHUNKS))(functools.partial(phases[which], chunk))
        return carry

    lax.fori_loop(0, CHUNKS + last, window, 0)


def to_rows(first, second):
    lane = lax.broadcasted_iota(jnp.int32, (ROWS, LANES), 1)
    tile = jnp.where(lane == 0, first, jnp.where(lane == 1, second, 0.0))
    if ROWS < LANES:
        tile = jnp.concatenate([tile, jnp.zeros((LANES - ROWS, LANES), F32)], axis=0)
    return tile.T[:8]


def kernel(
    acts,
    out_grad,
    wv,
    wo,
    decay,
    seg_out,
    seg_grad,
    value_grad,
    output_grad,
    hid,
    part,
    part_in,
    swap,
    swap_in,
    mixed,
    branch,
    branch_in,
    hid_out,
    out_land,
    grad,
    gpart,
    gpart_in,
    gswap,
    gswap_in,
    vgrad,
    gbranch,
    gbranch_in,
    grad_out,
    grad_land,
    stats,
    sums,
    sums_in,
    vals,
    norm,
    abx,
    aby,
    aby_in,
    table,
    tile,
    normed_t,
    mixed_t,
    recv,
    sent,
    once,
):
    p = lax.axis_index("pipe")
    d = lax.axis_index("dp")
    m = lax.axis_index("mp")
    x = d // 2
    z = d % 2
    (H_IN, ST_IN, P_IN, S_IN, M_IN, Y_IN, G_IN, GP_IN, GS_IN, V_IN, GY_IN, AX_IN, AY_IN) = range(13)
    (ST, PO, SW, MX, YO, HO, OO, GPO, GSW, VX, GYO, GO, GOO, AX, AY) = range(15)
    SUMS_R, OUT_R, GOUT_R, SUMS_S, FIRST_S = range(5)

    def cols_of(which):
        return pl.ds(pl.multiple_of(which * PIECE, LANES), PIECE)

    mine = pl.ds(pl.multiple_of(m * OWN, OWN), OWN)

    barrier = pltpu.get_barrier_semaphore()

    def greet(k, carry):
        dd = (d + k // 4) % 8
        mm = (m + k % 4) % 4
        pl.semaphore_signal(barrier, inc=1, device_id={"dp": dd, "mp": mm}, device_id_type=MESH)
        return carry

    lax.fori_loop(1, 32, greet, 0)

    @pl.when(p < SECTIONS - 1)
    def _():
        for k in range(4):
            pl.semaphore_signal(
                barrier, inc=1, device_id={"pipe": p + 1, "mp": (m + k) % 4}, device_id_type=MESH
            )

    @pl.when(p > 0)
    def _():
        for k in range(4):
            pl.semaphore_signal(
                barrier, inc=1, device_id={"pipe": p - 1, "mp": (m + k) % 4}, device_id_type=MESH
            )

    col_sum = jnp.sum(wv[0].astype(F32), axis=0, keepdims=True)
    sums[...] = jnp.broadcast_to(col_sum, (8, VAL))
    tile[...] = jnp.zeros((LANES, LANES), F32)
    row_id = lax.broadcasted_iota(jnp.int32, (MBT, MBT), 0).astype(F32)
    col_id = lax.broadcasted_iota(jnp.int32, (MBT, MBT), 1).astype(F32)
    for k in range(3):
        rate = jnp.full((MBT, MBT), decay[0, 3 * x + k], F32)
        scale = jnp.sqrt(1.0 - rate * rate)
        log_rate = jnp.log(rate)
        for way in range(2):
            offset = row_id - col_id if way == 0 else col_id - row_id
            power = jnp.exp(jnp.maximum(offset, 0.0) * log_rate) * scale
            table[way, k] = jnp.where(offset >= 0.0, power, 0.0).astype(BF16)

    inner = (p > 0) & (p < SECTIONS - 1)

    @pl.when(inner)
    def _():
        pl.semaphore_wait(barrier, 39)

    @pl.when(jnp.logical_not(inner))
    def _():
        pl.semaphore_wait(barrier, 35)

    def first_inputs(source, landing, sem):
        for b in range(2):
            start = (2 * d + b) * MBT
            chunk = start // ROWS
            row = pl.multiple_of(start % ROWS, MBT)
            for zz in range(2):
                for k in range(4):
                    dd = 2 * m + zz
                    mm = (m + k) % 4
                    send_or_copy(
                        (dd == d) & (mm == m),
                        source.at[b, :, pl.ds(zz * BLK, BLK)],
                        landing.at[chunk, pl.ds(row, MBT)],
                        once.at[FIRST_S],
                        recv.at[sem, chunk],
                        dp=dd,
                        mp=mm,
                    )

    @pl.when(p == 0)
    def _():
        first_inputs(acts, hid, H_IN)

    for k in range(1, 8):
        dd = (d + k) % 8
        send(
            sums.at[:, cols_of(dd // 2)],
            sums_in.at[k],
            once.at[SUMS_S],
            once.at[SUMS_R],
            dp=dd,
        )
    sums_in[0] = sums[:, cols_of(x)]

    @pl.when(p == SECTIONS - 1)
    def _():
        first_inputs(out_grad, grad, G_IN)

    await_bytes(sums_in.at[pl.ds(1, 7)], once.at[SUMS_R])

    def spread_pieces(c, source, landing, put, sem):
        for k in (2, 1, 3):
            send(
                source.at[c, k],
                landing.at[c, k - 1],
                sent.at[put, c],
                recv.at[sem, c],
                dp=2 * ((x + k) % 4) + z,
            )

    def gather_pieces(c, source, put, sem):
        for k in (2, 1, 3):
            send(
                source.at[c, x],
                source.at[c, x],
                sent.at[put, c],
                recv.at[sem, c],
                dp=2 * ((x + k) % 4) + z,
            )

    def spread_rows(c, source, landing, put, sem):
        for k in (2, 1, 3):
            mm = (m + k) % 4
            send(
                source.at[c, pl.ds(pl.multiple_of(mm * OWN, OWN), OWN)],
                landing.at[c, k - 1],
                sent.at[put, c],
                recv.at[sem, c],
                mp=mm,
            )

    def hand_on(c, source, landing, put, sem, to):
        for k in (2, 1, 3, 0):
            send(
                source.at[c],
                landing.at[c, mine],
                sent.at[put, c],
                recv.at[sem, c],
                pipe=to,
                mp=(m + k) % 4,
            )

    def deliver(c, source, landing, put, sem):
        start = c * ROWS
        dd = start // 128
        row = pl.multiple_of(start % 128 + m * OWN, OWN)
        send_or_copy(
            (dd == d) & (x == m),
            source.at[c],
            landing.at[pl.ds(row, OWN), pl.ds(pl.multiple_of(z * BLK, LANES), BLK)],
            sent.at[put, c],
            once.at[sem],
            dp=dd,
            mp=x,
        )

    def total_pieces(c, own, others):
        return (own[c, 0].astype(F32) + others[c, 0].astype(F32)) + (
            others[c, 1].astype(F32) + others[c, 2].astype(F32)
        )

    def total_rows(c, own, others):
        return (own[c, mine].astype(F32) + others[c, 0].astype(F32)) + (
            others[c, 1].astype(F32) + others[c, 2].astype(F32)
        )

    def forward_1(c):
        await_bytes(hid.at[c], recv.at[H_IN, c])
        here = hid[c]
        wide = here.astype(F32)
        mean = jnp.sum(wide, axis=1, keepdims=True) * (1.0 / BLK)
        centered = wide - mean
        stats[c, 0] = to_rows(mean, jnp.sum(centered * centered, axis=1, keepdims=True))
        for k in range(1, 8):
            send(
                stats.at[c, 0],
                stats.at[c, k],
                sent.at[ST, c],
                recv.at[ST_IN, c],
                dp=(d + k) % 8,
            )
        for k in (2, 1, 3, 0):
            cols = cols_of((x + k) % 4)
            product = jnp.dot(here, wv[0, :, cols], preferred_element_type=F32)
            part[c, k] = (product - mean * sums[0:1, cols]).astype(BF16)
        spread_pieces(c, part, part_in, PO, P_IN)

    def forward_2(c):
        await_bytes(part_in.at[c], recv.at[P_IN, c])
        total = total_pieces(c, part, part_in)
        vals[c] = total
        swap[c] = total.astype(BF16)
        send(swap.at[c], swap_in.at[c], sent.at[SW, c], recv.at[S_IN, c], dp=2 * x + 1 - z)

    def forward_3(c):
        await_bytes(stats.at[c, pl.ds(1, 7)], recv.at[ST_IN, c])
        means = [stats[c, k, 0:1, :] for k in range(8)]
        squares = [stats[c, k, 1:2, :] for k in range(8)]
        mean = functools.reduce(lambda a, b: a + b, means) * 0.125
        square = functools.reduce(lambda a, b: a + b, squares)
        for k in range(8):
            gap = means[k] - mean
            square = square + float(BLK) * gap * gap
            tile[k : k + 1, :] = gap
        tile[8:9, :] = mean
        tile[9:10, :] = lax.rsqrt(square * (1.0 / WIDTH) + EPSILON)
        columns = tile[...].T[:ROWS]
        norm[c] = columns
        shift = columns[:, 0:1] * sums_in[0, 0:1, :]
        for k in range(1, 8):
            shift = shift + columns[:, k : k + 1] * sums_in[k, 0:1, :]
        await_bytes(swap_in.at[c], recv.at[S_IN, c])
        value = (vals[c] + swap_in[c].astype(F32) + shift) * columns[:, 9:10]
        vals[c] = value
        rounded = value.astype(BF16)
        for b in range(ROWS // MBT):
            for k in range(3):
                mixed[c, x, b * MBT : (b + 1) * MBT, k * LANES : (k + 1) * LANES] = jnp.dot(
                    table[0, k],
                    rounded[b * MBT : (b + 1) * MBT, k * LANES : (k + 1) * LANES],
                    preferred_element_type=F32,
                ).astype(BF16)
        gather_pieces(c, mixed, MX, M_IN)

    def forward_4(c):
        await_bytes(mixed.at[c, pl.ds(0, 3)], recv.at[M_IN, c])
        whole = jnp.concatenate([mixed[c, k] for k in range(4)], axis=1)
        branch[c] = jnp.dot(whole, wo[0], preferred_element_type=F32).astype(BF16)
        spread_rows(c, branch, branch_in, YO, Y_IN)

    def forward_5(c):
        await_bytes(branch_in.at[c], recv.at[Y_IN, c])
        total = total_rows(c, branch, branch_in)
        hid_out[c] = (hid[c, mine].astype(F32) + total).astype(BF16)

        @pl.when(p < SECTIONS - 1)
        def _():
            hand_on(c, hid_out, hid, HO, H_IN, p + 1)

        deliver(c, hid_out, out_land, OO, OUT_R)

    run_phases(
        FORWARD_ORDER,
        {1: forward_1, 2: forward_2, 3: forward_3, 4: forward_4, 5: forward_5},
    )

    sum_all = sums_in[0, 0:1, :]
    for k in range(1, 8):
        sum_all = sum_all + sums_in[k, 0:1, :]
    sums_in[0, 0:1, :] = sum_all

    def backward_1(c):
        await_bytes(grad.at[c], recv.at[G_IN, c])
        here = grad[c]
        for k in (2, 1, 3, 0):
            rows = cols_of((x + k) % 4)
            gpart[c, k] = lax.dot_general(
                here, wo[0, rows, :], (((1,), (1,)), ((), ())), preferred_element_type=F32
            ).astype(BF16)
        spread_pieces(c, gpart, gpart_in, GPO, GP_IN)

    def backward_2(c):
        await_bytes(gpart_in.at[c], recv.at[GP_IN, c])
        gswap[c] = total_pieces(c, gpart, gpart_in).astype(BF16)
        send(gswap.at[c], gswap_in.at[c], sent.at[GSW, c], recv.at[GS_IN, c], dp=2 * x + 1 - z)

    def backward_3(c):
        await_bytes(gswap_in.at[c], recv.at[GS_IN, c])
        total = gswap[c].astype(F32) + gswap_in[c].astype(F32)
        rounded = total.astype(BF16)
        for b in range(ROWS // MBT):
            for k in range(3):
                vgrad[c, x, b * MBT : (b + 1) * MBT, k * LANES : (k + 1) * LANES] = jnp.dot(
                    table[1, k],
                    rounded[b * MBT : (b + 1) * MBT, k * LANES : (k + 1) * LANES],
                    preferred_element_type=F32,
                ).astype(BF16)
        gather_pieces(c, vgrad, VX, V_IN)
        wide = vgrad[c, x].astype(F32)
        abx[c, 0] = to_rows(
            jnp.sum(wide * sums_in[0, 0:1, :], axis=1, keepdims=True),
            jnp.sum(wide * vals[c], axis=1, keepdims=True),
        )
        for k in (2, 1, 3):
            send(
                abx.at[c, 0],
                abx.at[c, k],
                sent.at[AX, c],
                recv.at[AX_IN, c],
                dp=2 * ((x + k) % 4) + z,
            )

    def backward_4(c):
        await_bytes(abx.at[c, pl.ds(1, 3)], recv.at[AX_IN, c])
        aby[c] = (abx[c, 0] + abx[c, 1]) + (abx[c, 2] + abx[c, 3])
        for k in (2, 1, 3):
            send(aby.at[c], aby_in.at[c, k - 1], sent.at[AY, c], recv.at[AY_IN, c], mp=(m + k) % 4)
        await_bytes(vgrad.at[c, pl.ds(0, 3)], recv.at[V_IN, c])
        whole = jnp.concatenate([vgrad[c, k] for k in range(4)], axis=1)
        gbranch[c] = lax.dot_general(
            whole, wv[0], (((1,), (1,)), ((), ())), preferred_element_type=F32
        ).astype(BF16)
        spread_rows(c, gbranch, gbranch_in, GYO, GY_IN)

    def backward_5(c):
        await_bytes(aby_in.at[c], recv.at[AY_IN, c])
        tile[0:8, :] = ((aby[c] + aby_in[c, 0]) + (aby_in[c, 1] + aby_in[c, 2])) * (1.0 / WIDTH)
        tile[...] = tile[...].T
        means = tile[mine, :]
        columns = norm[c, mine, :]
        inverse = columns[:, 9:10]
        scaled = (hid[c, mine].astype(F32) - columns[:, 8:9]) * inverse
        await_bytes(gbranch_in.at[c], recv.at[GY_IN, c])
        total = total_rows(c, gbranch, gbranch_in)
        change = inverse * (total - means[:, 0:1] - scaled * means[:, 1:2])
        grad_out[c] = (grad[c, mine].astype(F32) + change).astype(BF16)

        @pl.when(p > 0)
        def _():
            hand_on(c, grad_out, grad, GO, G_IN, p - 1)

        deliver(c, grad_out, grad_land, GOO, GOUT_R)

    def transposed(c):
        start = pl.multiple_of(c * LANES, LANES)
        group = LANES // ROWS
        left = []
        for k in range(group):
            columns = norm[c * group + k]
            wide = hid[c * group + k].astype(F32)
            left.append((wide - columns[:, 8:9]) * columns[:, 9:10])
        normed = jnp.concatenate(left, axis=0).astype(BF16)
        normed_t[:, pl.ds(start, LANES)] = normed.T
        for x_at in range(4):
            rows = jnp.concatenate([mixed[c * group + k, x_at] for k in range(group)], axis=0)
            mixed_t[x_at * PIECE : (x_at + 1) * PIECE, pl.ds(start, LANES)] = rows.T

    @pl.loop(0, TOKENS // LANES)
    def _(c):
        transposed(c)

    run_phases(
        BACKWARD_ORDER,
        {1: backward_1, 2: backward_2, 3: backward_3, 4: backward_4, 5: backward_5},
    )

    whole_grad = grad[...].reshape(TOKENS, BLK)

    @pl.loop(0, 6)
    def _(k):
        rows = pl.ds(pl.multiple_of(k * 256, 256), 256)
        output_grad[0, rows, :] = jnp.dot(
            mixed_t[rows, :], whole_grad, preferred_element_type=F32
        ).astype(BF16)

    for x_at in range(4):
        right = vgrad[:, x_at].reshape(TOKENS, PIECE)

        @pl.loop(0, 3)
        def _(k):
            rows = pl.ds(pl.multiple_of(k * 256, 256), 256)
            value_grad[0, rows, x_at * PIECE : (x_at + 1) * PIECE] = jnp.dot(
                normed_t[rows, :], right, preferred_element_type=F32
            ).astype(BF16)

    await_bytes(out_land, once.at[OUT_R])
    seg_out[...] = out_land[...]
    await_bytes(grad_land, once.at[GOUT_R])
    seg_grad[...] = grad_land[...]

    await_bytes(sums_in.at[pl.ds(1, 7)], once.at[SUMS_S])

    @pl.when((p == 0) | (p == SECTIONS - 1))
    def _():
        for _ in range(14):
            await_bytes(acts.at[0, :, pl.ds(0, BLK)], once.at[FIRST_S])

        @pl.when(x != m)
        def _():
            for _ in range(2):
                await_bytes(acts.at[0, :, pl.ds(0, BLK)], once.at[FIRST_S])

    def drain(c, carry):
        await_bytes(stats.at[c, pl.ds(1, 7)], sent.at[ST, c])
        await_bytes(part_in.at[c], sent.at[PO, c])
        await_bytes(swap.at[c], sent.at[SW, c])
        await_bytes(mixed.at[c, pl.ds(0, 3)], sent.at[MX, c])
        await_bytes(branch_in.at[c], sent.at[YO, c])
        await_bytes(gpart_in.at[c], sent.at[GPO, c])
        await_bytes(gswap.at[c], sent.at[GSW, c])
        await_bytes(vgrad.at[c, pl.ds(0, 3)], sent.at[VX, c])
        await_bytes(gbranch_in.at[c], sent.at[GYO, c])
        await_bytes(abx.at[c, pl.ds(1, 3)], sent.at[AX, c])
        await_bytes(aby_in.at[c], sent.at[AY, c])

        @pl.when(p < SECTIONS - 1)
        def _():
            await_bytes(hid.at[c], sent.at[HO, c])

        @pl.when(p > 0)
        def _():
            await_bytes(grad.at[c], sent.at[GO, c])

        @pl.when(jnp.logical_not((c * ROWS // 128 == d) & (x == m)))
        def _():
            await_bytes(hid_out.at[c], sent.at[OO, c])
            await_bytes(grad_out.at[c], sent.at[GOO, c])

        return carry

    lax.fori_loop(0, CHUNKS, drain, 0)


def shards(acts, out_grad, value_weight, output_weight, decay):
    vmem = pl.BlockSpec(memory_space=pltpu.VMEM)
    way = [
        pltpu.VMEM((CHUNKS, ROWS, BLK), BF16),
        pltpu.VMEM((CHUNKS, 4, ROWS, PIECE), BF16),
        pltpu.VMEM((CHUNKS, 3, ROWS, PIECE), BF16),
        pltpu.VMEM((CHUNKS, ROWS, PIECE), BF16),
        pltpu.VMEM((CHUNKS, ROWS, PIECE), BF16),
        pltpu.VMEM((CHUNKS, 4, ROWS, PIECE), BF16),
        pltpu.VMEM((CHUNKS, ROWS, BLK), BF16),
        pltpu.VMEM((CHUNKS, 3, OWN, BLK), BF16),
        pltpu.VMEM((CHUNKS, OWN, BLK), BF16),
        pltpu.VMEM((128, VAL), BF16),
    ]
    scratch = [
        *way,
        *way,
        pltpu.VMEM((CHUNKS, 8, 8, LANES), F32),
        pltpu.VMEM((8, VAL), F32),
        pltpu.VMEM((8, 8, PIECE), F32),
        pltpu.VMEM((CHUNKS, ROWS, PIECE), F32),
        pltpu.VMEM((CHUNKS, ROWS, LANES), F32),
        pltpu.VMEM((CHUNKS, 4, 8, LANES), F32),
        pltpu.VMEM((CHUNKS, 8, LANES), F32),
        pltpu.VMEM((CHUNKS, 3, 8, LANES), F32),
        pltpu.VMEM((2, 3, MBT, MBT), BF16),
        pltpu.VMEM((LANES, LANES), F32),
        pltpu.VMEM((BLK, TOKENS), BF16),
        pltpu.VMEM((VAL, TOKENS), BF16),
        pltpu.SemaphoreType.DMA((13, CHUNKS)),
        pltpu.SemaphoreType.DMA((15, CHUNKS)),
        pltpu.SemaphoreType.DMA((5,)),
    ]
    flops = 6 * 2 * TOKENS * BLK * VAL
    seg_out, seg_grad, value_grad, output_grad = pl.pallas_call(
        kernel,
        out_shape=(
            jax.ShapeDtypeStruct((128, VAL), BF16),
            jax.ShapeDtypeStruct((128, VAL), BF16),
            jax.ShapeDtypeStruct((1, BLK, VAL), BF16),
            jax.ShapeDtypeStruct((1, VAL, BLK), BF16),
        ),
        in_specs=[vmem, vmem, vmem, vmem, pl.BlockSpec(memory_space=pltpu.SMEM)],
        out_specs=(vmem, vmem, vmem, vmem),
        scratch_shapes=scratch,
        compiler_params=pltpu.CompilerParams(
            collective_id=0, has_side_effects=True, vmem_limit_bytes=62 * 1024 * 1024
        ),
        cost_estimate=pl.CostEstimate(flops=flops, bytes_accessed=12_000_000, transcendentals=0),
    )(acts, out_grad, value_weight, output_weight, decay)
    shape = (1, 2, MBT, VAL)
    return seg_out.reshape(shape), seg_grad.reshape(shape), value_grad, output_grad


def solution(mesh):
    in_specs = (
        P("dp", None, "mp"),
        P("dp", None, "mp"),
        P("pipe", "dp", "mp"),
        P("pipe", "mp", "dp"),
        P("pipe", "mp"),
    )
    out_specs = (
        P("pipe", "dp", None, "mp"),
        P("pipe", "dp", None, "mp"),
        P("pipe", "dp", "mp"),
        P("pipe", "mp", "dp"),
    )
    return jax.shard_map(shards, mesh=mesh, in_specs=in_specs, out_specs=out_specs, check_vma=False)
```

time: 2240 us -> 679 us (0.30)
  waiting for transfers between devices: 1580 us -> 0 us
  Pallas kernels: 0 us -> 665 us
  blocking collectives: 324 us -> 0 us
  other arithmetic: 92.3 us -> 0 us
  matrix products: 90.1 us -> 0 us
  local copies, waits for them, and re-layouts: 83 us -> 8.31 us
  starting transfers between devices: 42.2 us -> 0 us
    all_gather x4 -> x0, waiting for transfers between devices: 836 us -> none  [the longest x1 336 us: shards(): lax.all_gather(output_weight[0], 'dp', axis=1, tiled=True)]
    reduce_scatter x18 -> x0, waiting for transfers between devices: 695 us -> none  [the longest x9 359 us: backward_step(): lax.psum_scatter(partial_grad.astype(jnp.bfloat16), 'mp', scatter_dimensi...]
    pallas_call x0 -> x1, Pallas kernels: none -> 665 us  [shards(): pl.pallas_call(kernel, out_shape=(jax.ShapeDtypeStruct((128, VAL), BF16),...]
    all_gather x18 -> x0, blocking collectives: 251 us -> none  [the longest x9 126 us: backward_step(): grad_whole = lax.all_gather(grad_in, 'mp', axis=1, tiled=True)]
    dot_general x14 -> x0, matrix products: 90.1 us -> none  [the longest x2 24.5 us: local_back(): jnp.einsum('tv,wv->tw', values_grad, weights_in, preferred_element_type=j...]
    psum x9 -> x0, blocking collectives: 73.6 us -> none  [backward_step(): lax.psum((jnp.sum(normed_grad, axis=1), jnp.sum(normed_grad * scaled, axi...]
    dynamic_update_slice x72 -> x0, other arithmetic: 65.4 us -> none  [place_row(): lax.dynamic_update_index_in_dim(buffer, jnp.where(active, value, previous...]
    dynamic_slice x63 -> x0, local copies, waits for them, and re-layouts: 37.6 us -> none  [fetch_row(): return lax.dynamic_index_in_dim(buffer, which, 0, keepdims=False)]
  transfers between devices with their start and end apart: 42 -> 0, of which waited for: 41 -> 0; matrix products, arithmetic and copies ran while one was open for 3% -> 0% of each run, Pallas kernels for 0% -> 0%
where the time goes in v1:
time: 679 us; the launch traced here: 674 us
  Pallas kernels  665 us (98%)
  local copies, waits for them, and re-layouts  8.31 us (1%)
    pallas_call x1, Pallas kernels, shards(): pl.pallas_call(kernel, out_shape=(jax.ShapeDtypeStruct((128, VAL), BF16),...  665 us

profile of v1, /device:TPU:134, one launch (start us, length us, event | category | flops | bytes accessed | tf_op | source)
XLA Modules:
  0.0 673.6 jit_solution(1685080668848119845)
XLA Ops:
  0.6 664.7 %shard_map.84 = (bf16[128,1536]{1,0:T(8,128)(2,1)}, bf16[128,1536]{1,0:T(8,128)(2,1)}, bf16[1,768,1536]{2,1,0:T(8,128)(2,1)}, bf16[1,1536,768]{2,1,0:T(8,128)(2,1)}) custom-call(bf16[2,64,1536]{2,1,0:T(8,128)(2,1)} %acts.1, bf16[2,64,1536]{2,1,0:T(8,128)(2,1)} %out_grad.1, bf16[1,768,1536]{2,1,0:T(8,128)(2,1)} %wv.1, bf16[1,1536,768]{2,1,0:T(8,128)(2,1)} %wo.1, ...), custom_call_target="tpu_custom_call" | custom-call | flops 14495514624 | bytes 12000000 | tf_op jit(solution)/shard_map/pallas_call | solution.py:571
  665.3 1.8 copy.13
  667.1 1.8 copy.14
  668.9 0.0 copy-start
  668.9 3.4 copy.15
  672.2 0.0 copy-done
  672.2 1.4 copy.16
Async XLA Ops:
  668.9 3.4 copy-start

commit v2 on v1

--- a/solution.py
+++ b/solution.py
@@ -24,8 +24,8 @@
 SECTIONS = 8
 LANES = 128
 
-FORWARD_ORDER = ((1, 0), (3, 1), (5, 2), (2, 0), (4, 1))
-BACKWARD_ORDER = ((1, 0), (3, 1), (5, 2), (2, 0), (4, 1))
+LAST_FORWARD = 20
+BACKWARD_START = (12, 21, 21)
 
 
 def send(src, dst, send_sem, recv_sem, **device):
@@ -51,18 +51,6 @@
     @pl.when(jnp.logical_not(here))
     def _():
         send(src, dst, send_sem, recv_sem, **device)
-
-
-def run_phases(order, phases):
-    last = max(lag for _, lag in order)
-
-    def window(step, carry):
-        for which, lag in order:
-            chunk = step - lag
-            pl.when((chunk >= 0) & (chunk < CHUNKS))(functools.partial(phases[which], chunk))
-        return carry
-
-    lax.fori_loop(0, CHUNKS + last, window, 0)
 
 
 def to_rows(first, second):
@@ -106,6 +94,7 @@
     stats,
     sums,
     sums_in,
+    sums_all,
     vals,
     norm,
     abx,
@@ -220,16 +209,19 @@
         first_inputs(out_grad, grad, G_IN)
 
     await_bytes(sums_in.at[pl.ds(1, 7)], once.at[SUMS_R])
-
-    def spread_pieces(c, source, landing, put, sem):
-        for k in (2, 1, 3):
-            send(
-                source.at[c, k],
-                landing.at[c, k - 1],
-                sent.at[put, c],
-                recv.at[sem, c],
-                dp=2 * ((x + k) % 4) + z,
-            )
+    sum_all = sums_in[0]
+    for k in range(1, 8):
+        sum_all = sum_all + sums_in[k]
+    sums_all[...] = sum_all
+
+    def spread_piece(c, k, source, landing, put, sem):
+        send(
+            source.at[c, k],
+            landing.at[c, k - 1],
+            sent.at[put, c],
+            recv.at[sem, c],
+            dp=2 * ((x + k) % 4) + z,
+        )
 
     def gather_pieces(c, source, put, sem):
         for k in (2, 1, 3):
@@ -287,26 +279,49 @@
             others[c, 1].astype(F32) + others[c, 2].astype(F32)
         )
 
+    def means_1(c):
+        wide = vgrad[c, x].astype(F32)
+        abx[c, 0] = to_rows(
+            jnp.sum(wide * sums_all[0:1, :], axis=1, keepdims=True),
+            jnp.sum(wide * vals[c], axis=1, keepdims=True),
+        )
+        for k in (2, 1, 3):
+            send(
+                abx.at[c, 0],
+                abx.at[c, k],
+                sent.at[AX, c],
+                recv.at[AX_IN, c],
+                dp=2 * ((x + k) % 4) + z,
+            )
+
+    def means_2(c):
+        await_bytes(abx.at[c, pl.ds(1, 3)], recv.at[AX_IN, c])
+        aby[c] = (abx[c, 0] + abx[c, 1]) + (abx[c, 2] + abx[c, 3])
+        for k in (2, 1, 3):
+            send(aby.at[c], aby_in.at[c, k - 1], sent.at[AY, c], recv.at[AY_IN, c], mp=(m + k) % 4)
+
     def forward_1(c):
         await_bytes(hid.at[c], recv.at[H_IN, c])
         here = hid[c]
         wide = here.astype(F32)
         mean = jnp.sum(wide, axis=1, keepdims=True) * (1.0 / BLK)
         centered = wide - mean
-        stats[c, 0] = to_rows(mean, jnp.sum(centered * centered, axis=1, keepdims=True))
-        for k in range(1, 8):
-            send(
-                stats.at[c, 0],
-                stats.at[c, k],
-                sent.at[ST, c],
-                recv.at[ST_IN, c],
-                dp=(d + k) % 8,
-            )
         for k in (2, 1, 3, 0):
             cols = cols_of((x + k) % 4)
             product = jnp.dot(here, wv[0, :, cols], preferred_element_type=F32)
             part[c, k] = (product - mean * sums[0:1, cols]).astype(BF16)
-        spread_pieces(c, part, part_in, PO, P_IN)
+            if k:
+                spread_piece(c, k, part, part_in, PO, P_IN)
+            if k == 1:
+                stats[c, 0] = to_rows(mean, jnp.sum(centered * centered, axis=1, keepdims=True))
+                for j in range(1, 8):
+                    send(
+                        stats.at[c, 0],
+                        stats.at[c, j],
+                        sent.at[ST, c],
+                        recv.at[ST_IN, c],
+                        dp=(d + j) % 8,
+                    )
 
     def forward_2(c):
         await_bytes(part_in.at[c], recv.at[P_IN, c])
@@ -344,12 +359,14 @@
                     preferred_element_type=F32,
                 ).astype(BF16)
         gather_pieces(c, mixed, MX, M_IN)
+        pl.when(p == SECTIONS - 1)(functools.partial(means_1, c))
 
     def forward_4(c):
         await_bytes(mixed.at[c, pl.ds(0, 3)], recv.at[M_IN, c])
         whole = jnp.concatenate([mixed[c, k] for k in range(4)], axis=1)
         branch[c] = jnp.dot(whole, wo[0], preferred_element_type=F32).astype(BF16)
         spread_rows(c, branch, branch_in, YO, Y_IN)
+        pl.when(p == SECTIONS - 1)(functools.partial(means_2, c))
 
     def forward_5(c):
         await_bytes(branch_in.at[c], recv.at[Y_IN, c])
@@ -361,16 +378,6 @@
             hand_on(c, hid_out, hid, HO, H_IN, p + 1)
 
         deliver(c, hid_out, out_land, OO, OUT_R)
-
-    run_phases(
-        FORWARD_ORDER,
-        {1: forward_1, 2: forward_2, 3: forward_3, 4: forward_4, 5: forward_5},
-    )
-
-    sum_all = sums_in[0, 0:1, :]
-    for k in range(1, 8):
-        sum_all = sum_all + sums_in[k, 0:1, :]
-    sums_in[0, 0:1, :] = sum_all
 
     def backward_1(c):
         await_bytes(grad.at[c], recv.at[G_IN, c])
@@ -380,7 +387,8 @@
             gpart[c, k] = lax.dot_general(
                 here, wo[0, rows, :], (((1,), (1,)), ((), ())), preferred_element_type=F32
             ).astype(BF16)
-        spread_pieces(c, gpart, gpart_in, GPO, GP_IN)
+            if k:
+                spread_piece(c, k, gpart, gpart_in, GPO, GP_IN)
 
     def backward_2(c):
         await_bytes(gpart_in.at[c], recv.at[GP_IN, c])
@@ -399,31 +407,16 @@
                     preferred_element_type=F32,
                 ).astype(BF16)
         gather_pieces(c, vgrad, VX, V_IN)
-        wide = vgrad[c, x].astype(F32)
-        abx[c, 0] = to_rows(
-            jnp.sum(wide * sums_in[0, 0:1, :], axis=1, keepdims=True),
-            jnp.sum(wide * vals[c], axis=1, keepdims=True),
-        )
-        for k in (2, 1, 3):
-            send(
-                abx.at[c, 0],
-                abx.at[c, k],
-                sent.at[AX, c],
-                recv.at[AX_IN, c],
-                dp=2 * ((x + k) % 4) + z,
-            )
+        pl.when(p < SECTIONS - 1)(functools.partial(means_1, c))
 
     def backward_4(c):
-        await_bytes(abx.at[c, pl.ds(1, 3)], recv.at[AX_IN, c])
-        aby[c] = (abx[c, 0] + abx[c, 1]) + (abx[c, 2] + abx[c, 3])
-        for k in (2, 1, 3):
-            send(aby.at[c], aby_in.at[c, k - 1], sent.at[AY, c], recv.at[AY_IN, c], mp=(m + k) % 4)
         await_bytes(vgrad.at[c, pl.ds(0, 3)], recv.at[V_IN, c])
         whole = jnp.concatenate([vgrad[c, k] for k in range(4)], axis=1)
         gbranch[c] = lax.dot_general(
             whole, wv[0], (((1,), (1,)), ((), ())), preferred_element_type=F32
         ).astype(BF16)
         spread_rows(c, gbranch, gbranch_in, GYO, GY_IN)
+        pl.when(p < SECTIONS - 1)(functools.partial(means_2, c))
 
     def backward_5(c):
         await_bytes(aby_in.at[c], recv.at[AY_IN, c])
@@ -458,14 +451,38 @@
             rows = jnp.concatenate([mixed[c * group + k, x_at] for k in range(group)], axis=0)
             mixed_t[x_at * PIECE : (x_at + 1) * PIECE, pl.ds(start, LANES)] = rows.T
 
-    @pl.loop(0, TOKENS // LANES)
-    def _(c):
-        transposed(c)
-
-    run_phases(
-        BACKWARD_ORDER,
-        {1: backward_1, 2: backward_2, 3: backward_3, 4: backward_4, 5: backward_5},
+    def transposed_2(c):
+        pl.when(c % (LANES // ROWS) == LANES // ROWS - 1)(
+            functools.partial(transposed, c // (LANES // ROWS))
+        )
+
+    is_last = p == SECTIONS - 1
+    ahead = jnp.where(is_last, LAST_FORWARD, 0)
+    near, middle, far = BACKWARD_START
+    behind = jnp.where(p == SECTIONS - 2, near, jnp.where(p == SECTIONS - 3, middle, far))
+    start = jnp.where(is_last, 0, behind)
+    finish = jnp.where(is_last, LAST_FORWARD, behind) + 4
+    phases = (
+        (forward_1, ahead),
+        (forward_2, ahead + 1),
+        (forward_3, ahead + 2),
+        (forward_4, ahead + 3),
+        (forward_5, ahead + 4),
+        (transposed_2, ahead + 4),
+        (backward_1, start),
+        (backward_2, start + 1),
+        (backward_3, start + 2),
+        (backward_4, start + 3),
+        (backward_5, finish),
     )
+
+    def window(step, carry):
+        for phase, lag in phases:
+            chunk = step - lag
+            pl.when((chunk >= 0) & (chunk < CHUNKS))(functools.partial(phase, chunk))
+        return carry
+
+    lax.fori_loop(0, finish + CHUNKS, window, 0)
 
     whole_grad = grad[...].reshape(TOKENS, BLK)
 
@@ -554,6 +571,7 @@
         pltpu.VMEM((CHUNKS, 8, 8, LANES), F32),
         pltpu.VMEM((8, VAL), F32),
         pltpu.VMEM((8, 8, PIECE), F32),
+        pltpu.VMEM((8, PIECE), F32),
         pltpu.VMEM((CHUNKS, ROWS, PIECE), F32),
         pltpu.VMEM((CHUNKS, ROWS, LANES), F32),
         pltpu.VMEM((CHUNKS, 4, 8, LANES), F32),

time: 679 us -> 570 us (0.84)
  Pallas kernels: 665 us -> 555 us
    pallas_call x1, Pallas kernels: 665 us -> 555 us  [shards(): pl.pallas_call(kernel, out_shape=(jax.ShapeDtypeStruct((128, VAL), BF16),...]
where the time goes in v2:
time: 570 us; the launch traced here: 564 us
  Pallas kernels  555 us (97%)
  local copies, waits for them, and re-layouts  8.31 us (1%)
    pallas_call x1, Pallas kernels, shards(): pl.pallas_call(kernel, out_shape=(jax.ShapeDtypeStruct((128, VAL), BF16),...  555 us

profile of v2, /device:TPU:134, one launch (start us, length us, event | category | flops | bytes accessed | tf_op | source)
XLA Modules:
  0.0 564.4 jit_solution(5670871476994967945)
XLA Ops:
  0.6 555.4 %shard_map.84 = (bf16[128,1536]{1,0:T(8,128)(2,1)}, bf16[128,1536]{1,0:T(8,128)(2,1)}, bf16[1,768,1536]{2,1,0:T(8,128)(2,1)}, bf16[1,1536,768]{2,1,0:T(8,128)(2,1)}) custom-call(bf16[2,64,1536]{2,1,0:T(8,128)(2,1)} %acts.1, bf16[2,64,1536]{2,1,0:T(8,128)(2,1)} %out_grad.1, bf16[1,768,1536]{2,1,0:T(8,128)(2,1)} %wv.1, bf16[1,1536,768]{2,1,0:T(8,128)(2,1)} %wo.1, ...), custom_call_target="tpu_custom_call" | custom-call | flops 14495514624 | bytes 12000000 | tf_op jit(solution)/shard_map/pallas_call | solution.py:589
  556.1 1.8 copy.13
  557.8 1.8 copy.14
  559.6 0.0 copy-start
  559.6 3.4 copy.15
  563.0 0.0 copy-done
  563.0 1.4 copy.16
Async XLA Ops:
  559.6 3.4 copy-start

commit v3 on v2

--- a/solution.py
+++ b/solution.py
@@ -25,7 +25,8 @@
 LANES = 128
 
 LAST_FORWARD = 20
-BACKWARD_START = (12, 21, 21)
+RELAY_AHEAD = 2
+BACKWARD_START = (11, 20, 20)
 
 
 def send(src, dst, send_sem, recv_sem, **device):
@@ -104,6 +105,8 @@
     tile,
     normed_t,
     mixed_t,
+    wv_t,
+    wo_t,
     recv,
     sent,
     once,
@@ -114,7 +117,7 @@
     x = d // 2
     z = d % 2
     (H_IN, ST_IN, P_IN, S_IN, M_IN, Y_IN, G_IN, GP_IN, GS_IN, V_IN, GY_IN, AX_IN, AY_IN) = range(13)
-    (ST, PO, SW, MX, YO, HO, OO, GPO, GSW, VX, GYO, GO, GOO, AX, AY) = range(15)
+    (ST, PO, SW, MX, YO, HO, OO, GPO, GSW, VX, GYO, GO, GOO, AX, AY, RL) = range(16)
     SUMS_R, OUT_R, GOUT_R, SUMS_S, FIRST_S = range(5)
 
     def cols_of(which):
@@ -170,13 +173,13 @@
     def _():
         pl.semaphore_wait(barrier, 35)
 
-    def first_inputs(source, landing, sem):
+    def first_inputs(source, landing, sem, rows):
         for b in range(2):
             start = (2 * d + b) * MBT
             chunk = start // ROWS
             row = pl.multiple_of(start % ROWS, MBT)
             for zz in range(2):
-                for k in range(4):
+                for k in range(rows):
                     dd = 2 * m + zz
                     mm = (m + k) % 4
                     send_or_copy(
@@ -189,10 +192,6 @@
                         mp=mm,
                     )
 
-    @pl.when(p == 0)
-    def _():
-        first_inputs(acts, hid, H_IN)
-
     for k in range(1, 8):
         dd = (d + k) % 8
         send(
@@ -204,15 +203,20 @@
         )
     sums_in[0] = sums[:, cols_of(x)]
 
+    @pl.when(p == 0)
+    def _():
+        first_inputs(acts, hid, H_IN, 1)
+
     @pl.when(p == SECTIONS - 1)
     def _():
-        first_inputs(out_grad, grad, G_IN)
-
-    await_bytes(sums_in.at[pl.ds(1, 7)], once.at[SUMS_R])
-    sum_all = sums_in[0]
-    for k in range(1, 8):
-        sum_all = sum_all + sums_in[k]
-    sums_all[...] = sum_all
+        first_inputs(out_grad, grad, G_IN, 4)
+
+    def whole_sums():
+        await_bytes(sums_in.at[pl.ds(1, 7)], once.at[SUMS_R])
+        sum_all = sums_in[0]
+        for k in range(1, 8):
+            sum_all = sum_all + sums_in[k]
+        sums_all[...] = sum_all
 
     def spread_piece(c, k, source, landing, put, sem):
         send(
@@ -300,8 +304,40 @@
         for k in (2, 1, 3):
             send(aby.at[c], aby_in.at[c, k - 1], sent.at[AY, c], recv.at[AY_IN, c], mp=(m + k) % 4)
 
+    def flip():
+        @pl.loop(0, VAL // LANES)
+        def _(k):
+            at = pl.ds(pl.multiple_of(k * LANES, LANES), LANES)
+            wo_t[:, at] = wo[0, at, :].T
+            wv_t[at, :] = wv[0, :, at].T
+
+    pl.when(p > 0)(flip)
+
+    relays = (p == 0) & (x == m)
+
+    def relay(c):
+        await_bytes(hid.at[c], recv.at[H_IN, c])
+        for k in (2, 1, 3):
+            send(
+                hid.at[c],
+                hid.at[c],
+                sent.at[RL, c],
+                recv.at[H_IN, c],
+                mp=(m + k) % 4,
+            )
+
+    @pl.when(relays)
+    def _():
+        for c in range(RELAY_AHEAD):
+            relay(c)
+
     def forward_1(c):
-        await_bytes(hid.at[c], recv.at[H_IN, c])
+        pl.when(relays & (c < CHUNKS - RELAY_AHEAD))(functools.partial(relay, c + RELAY_AHEAD))
+
+        @pl.when(jnp.logical_not(relays))
+        def _():
+            await_bytes(hid.at[c], recv.at[H_IN, c])
+
         here = hid[c]
         wide = here.astype(F32)
         mean = jnp.sum(wide, axis=1, keepdims=True) * (1.0 / BLK)
@@ -331,6 +367,7 @@
         send(swap.at[c], swap_in.at[c], sent.at[SW, c], recv.at[S_IN, c], dp=2 * x + 1 - z)
 
     def forward_3(c):
+        pl.when(c == 0)(whole_sums)
         await_bytes(stats.at[c, pl.ds(1, 7)], recv.at[ST_IN, c])
         means = [stats[c, k, 0:1, :] for k in range(8)]
         squares = [stats[c, k, 1:2, :] for k in range(8)]
@@ -379,13 +416,33 @@
 
         deliver(c, hid_out, out_land, OO, OUT_R)
 
+    def output_weights():
+        @pl.loop(0, 6)
+        def _(k):
+            rows = pl.ds(pl.multiple_of(k * 256, 256), 256)
+            output_grad[0, rows, :] = jnp.dot(
+                mixed_t[rows, :], grad[...].reshape(TOKENS, BLK), preferred_element_type=F32
+            ).astype(BF16)
+
+    def value_weights():
+        for x_at in range(4):
+
+            @pl.loop(0, 3)
+            def _(k):
+                rows = pl.ds(pl.multiple_of(k * 256, 256), 256)
+                value_grad[0, rows, x_at * PIECE : (x_at + 1) * PIECE] = jnp.dot(
+                    normed_t[rows, :],
+                    vgrad[:, x_at].reshape(TOKENS, PIECE),
+                    preferred_element_type=F32,
+                ).astype(BF16)
+
     def backward_1(c):
         await_bytes(grad.at[c], recv.at[G_IN, c])
         here = grad[c]
         for k in (2, 1, 3, 0):
-            rows = cols_of((x + k) % 4)
-            gpart[c, k] = lax.dot_general(
-                here, wo[0, rows, :], (((1,), (1,)), ((), ())), preferred_element_type=F32
+            cols = cols_of((x + k) % 4)
+            gpart[c, k] = jnp.dot(
+                here, wo_t[:, cols], preferred_element_type=F32
             ).astype(BF16)
             if k:
                 spread_piece(c, k, gpart, gpart_in, GPO, GP_IN)
@@ -394,6 +451,7 @@
         await_bytes(gpart_in.at[c], recv.at[GP_IN, c])
         gswap[c] = total_pieces(c, gpart, gpart_in).astype(BF16)
         send(gswap.at[c], gswap_in.at[c], sent.at[GSW, c], recv.at[GS_IN, c], dp=2 * x + 1 - z)
+        pl.when((p == 0) & (c == CHUNKS - 1))(output_weights)
 
     def backward_3(c):
         await_bytes(gswap_in.at[c], recv.at[GS_IN, c])
@@ -412,11 +470,10 @@
     def backward_4(c):
         await_bytes(vgrad.at[c, pl.ds(0, 3)], recv.at[V_IN, c])
         whole = jnp.concatenate([vgrad[c, k] for k in range(4)], axis=1)
-        gbranch[c] = lax.dot_general(
-            whole, wv[0], (((1,), (1,)), ((), ())), preferred_element_type=F32
-        ).astype(BF16)
+        gbranch[c] = jnp.dot(whole, wv_t[...], preferred_element_type=F32).astype(BF16)
         spread_rows(c, gbranch, gbranch_in, GYO, GY_IN)
         pl.when(p < SECTIONS - 1)(functools.partial(means_2, c))
+        pl.when((p == 0) & (c == CHUNKS - 1))(value_weights)
 
     def backward_5(c):
         await_bytes(aby_in.at[c], recv.at[AY_IN, c])
@@ -477,6 +534,7 @@
     )
 
     def window(step, carry):
+        pl.when((p == 0) & (step == CHUNKS + 4))(flip)
         for phase, lag in phases:
             chunk = step - lag
             pl.when((chunk >= 0) & (chunk < CHUNKS))(functools.partial(phase, chunk))
@@ -484,41 +542,25 @@
 
     lax.fori_loop(0, finish + CHUNKS, window, 0)
 
-    whole_grad = grad[...].reshape(TOKENS, BLK)
-
-    @pl.loop(0, 6)
-    def _(k):
-        rows = pl.ds(pl.multiple_of(k * 256, 256), 256)
-        output_grad[0, rows, :] = jnp.dot(
-            mixed_t[rows, :], whole_grad, preferred_element_type=F32
-        ).astype(BF16)
-
-    for x_at in range(4):
-        right = vgrad[:, x_at].reshape(TOKENS, PIECE)
-
-        @pl.loop(0, 3)
-        def _(k):
-            rows = pl.ds(pl.multiple_of(k * 256, 256), 256)
-            value_grad[0, rows, x_at * PIECE : (x_at + 1) * PIECE] = jnp.dot(
-                normed_t[rows, :], right, preferred_element_type=F32
-            ).astype(BF16)
+    pl.when(p > 0)(output_weights)
+    pl.when(p > 0)(value_weights)
 
     await_bytes(out_land, once.at[OUT_R])
-    seg_out[...] = out_land[...]
+    for b in range(2):
+        seg_out[0, b] = out_land[b * MBT : (b + 1) * MBT]
     await_bytes(grad_land, once.at[GOUT_R])
-    seg_grad[...] = grad_land[...]
+    for b in range(2):
+        seg_grad[0, b] = grad_land[b * MBT : (b + 1) * MBT]
 
     await_bytes(sums_in.at[pl.ds(1, 7)], once.at[SUMS_S])
 
-    @pl.when((p == 0) | (p == SECTIONS - 1))
-    def _():
-        for _ in range(14):
+    def first_sent(count):
+        for _ in range(count):
             await_bytes(acts.at[0, :, pl.ds(0, BLK)], once.at[FIRST_S])
 
-        @pl.when(x != m)
-        def _():
-            for _ in range(2):
-                await_bytes(acts.at[0, :, pl.ds(0, BLK)], once.at[FIRST_S])
+    pl.when(p == 0)(functools.partial(first_sent, 2))
+    pl.when(p == SECTIONS - 1)(functools.partial(first_sent, 14))
+    pl.when(((p == 0) | (p == SECTIONS - 1)) & (x != m))(functools.partial(first_sent, 2))
 
     def drain(c, carry):
         await_bytes(stats.at[c, pl.ds(1, 7)], sent.at[ST, c])
@@ -532,6 +574,11 @@
         await_bytes(gbranch_in.at[c], sent.at[GYO, c])
         await_bytes(abx.at[c, pl.ds(1, 3)], sent.at[AX, c])
         await_bytes(aby_in.at[c], sent.at[AY, c])
+
+        @pl.when(relays)
+        def _():
+            for _ in range(3):
+                await_bytes(hid.at[c], sent.at[RL, c])
 
         @pl.when(p < SECTIONS - 1)
         def _():
@@ -581,16 +628,18 @@
         pltpu.VMEM((LANES, LANES), F32),
         pltpu.VMEM((BLK, TOKENS), BF16),
         pltpu.VMEM((VAL, TOKENS), BF16),
+        pltpu.VMEM((VAL, BLK), BF16),
+        pltpu.VMEM((BLK, VAL), BF16),
         pltpu.SemaphoreType.DMA((13, CHUNKS)),
-        pltpu.SemaphoreType.DMA((15, CHUNKS)),
+        pltpu.SemaphoreType.DMA((16, CHUNKS)),
         pltpu.SemaphoreType.DMA((5,)),
     ]
     flops = 6 * 2 * TOKENS * BLK * VAL
-    seg_out, seg_grad, value_grad, output_grad = pl.pallas_call(
+    return pl.pallas_call(
         kernel,
         out_shape=(
-            jax.ShapeDtypeStruct((128, VAL), BF16),
-            jax.ShapeDtypeStruct((128, VAL), BF16),
+            jax.ShapeDtypeStruct((1, 2, MBT, VAL), BF16),
+            jax.ShapeDtypeStruct((1, 2, MBT, VAL), BF16),
             jax.ShapeDtypeStruct((1, BLK, VAL), BF16),
             jax.ShapeDtypeStruct((1, VAL, BLK), BF16),
         ),
@@ -602,8 +651,6 @@
         ),
         cost_estimate=pl.CostEstimate(flops=flops, bytes_accessed=12_000_000, transcendentals=0),
     )(acts, out_grad, value_weight, output_weight, decay)
-    shape = (1, 2, MBT, VAL)
-    return seg_out.reshape(shape), seg_grad.reshape(shape), value_grad, output_grad
 
 
 def solution(mesh):

time: 570 us -> 538 us (0.944)
  Pallas kernels: 555 us -> 529 us
    pallas_call x1, Pallas kernels: 555 us -> 529 us  [shards(): pl.pallas_call(kernel, out_shape=(jax.ShapeDtypeStruct((1, 2, MBT, VAL),...]
where the time goes in v3:
time: 538 us
  Pallas kernels  529 us (98%)
  local copies, waits for them, and re-layouts  8.31 us (2%)
    pallas_call x1, Pallas kernels, shards(): pl.pallas_call(kernel, out_shape=(jax.ShapeDtypeStruct((1, 2, MBT, VAL),...  529 us

profile of v3, /device:TPU:134, one launch (start us, length us, event | category | flops | bytes accessed | tf_op | source)
XLA Modules:
  0.0 538.1 jit_solution(1648325643822293341)
XLA Ops:
  0.6 529.1 %shard_map.84 = (bf16[1,2,64,1536]{3,2,1,0:T(8,128)(2,1)}, bf16[1,2,64,1536]{3,2,1,0:T(8,128)(2,1)}, bf16[1,768,1536]{2,1,0:T(8,128)(2,1)}, bf16[1,1536,768]{2,1,0:T(8,128)(2,1)}) custom-call(bf16[2,64,1536]{2,1,0:T(8,128)(2,1)} %acts.1, bf16[2,64,1536]{2,1,0:T(8,128)(2,1)} %out_grad.1, bf16[1,768,1536]{2,1,0:T(8,128)(2,1)} %wv.1, bf16[1,1536,768]{2,1,0:T(8,128)(2,1)} %wo.1, ...), custom_call_target="tpu_custom_call" | custom-call | flops 14495514624 | bytes 12000000 | tf_op jit(solution)/shard_map/pallas_call | solution.py:638
  529.8 1.8 copy.13
  531.5 1.8 copy.14
  533.3 0.0 copy-start
  533.3 3.4 copy.15
  536.7 0.0 copy-done
  536.7 1.4 copy.16
Async XLA Ops:
  533.3 3.4 copy-start

commit v4 on v3

--- a/solution.py
+++ b/solution.py
@@ -520,17 +520,17 @@
     start = jnp.where(is_last, 0, behind)
     finish = jnp.where(is_last, LAST_FORWARD, behind) + 4
     phases = (
+        (backward_1, start),
+        (backward_2, start + 1),
+        (backward_3, start + 2),
+        (backward_4, start + 3),
+        (backward_5, finish),
         (forward_1, ahead),
         (forward_2, ahead + 1),
         (forward_3, ahead + 2),
         (forward_4, ahead + 3),
         (forward_5, ahead + 4),
         (transposed_2, ahead + 4),
-        (backward_1, start),
-        (backward_2, start + 1),
-        (backward_3, start + 2),
-        (backward_4, start + 3),
-        (backward_5, finish),
     )
 
     def window(step, carry):

time: 538 us -> 537 us (level)
  no operation moved by 1% of the time
where the time goes in v4:
time: 537 us; the launch traced here: 536 us
  Pallas kernels  527 us (98%)
  local copies, waits for them, and re-layouts  8.31 us (2%)
    pallas_call x1, Pallas kernels, shards(): pl.pallas_call(kernel, out_shape=(jax.ShapeDtypeStruct((1, 2, MBT, VAL),...  527 us

profile of v4, /device:TPU:134, one launch (start us, length us, event | category | flops | bytes accessed | tf_op | source)
XLA Modules:
  0.0 535.6 jit_solution(8474514192052146070)
XLA Ops:
  0.6 526.6 %shard_map.84 = (bf16[1,2,64,1536]{3,2,1,0:T(8,128)(2,1)}, bf16[1,2,64,1536]{3,2,1,0:T(8,128)(2,1)}, bf16[1,768,1536]{2,1,0:T(8,128)(2,1)}, bf16[1,1536,768]{2,1,0:T(8,128)(2,1)}) custom-call(bf16[2,64,1536]{2,1,0:T(8,128)(2,1)} %acts.1, bf16[2,64,1536]{2,1,0:T(8,128)(2,1)} %out_grad.1, bf16[1,768,1536]{2,1,0:T(8,128)(2,1)} %wv.1, bf16[1,1536,768]{2,1,0:T(8,128)(2,1)} %wo.1, ...), custom_call_target="tpu_custom_call" | custom-call | flops 14495514624 | bytes 12000000 | tf_op jit(solution)/shard_map/pallas_call | solution.py:638
  527.3 1.8 copy.13
  529.0 1.8 copy.14
  530.8 0.0 copy-start
  530.8 3.4 copy.15
  534.2 0.0 copy-done
  534.2 1.4 copy.16
Async XLA Ops:
  530.8 3.4 copy-start
